TPU v7x, 512 devices: a whole 4x8x8 slice. The times are simulated.
512 devices in a mesh: row: 64 (over z, y_hi, core), col: 8 (over y_lo, x).
Axes of the slice: x: 4, y: 8 (y_hi: 4, y_lo: 2; y = y_hi * 2 + y_lo), z: 8, core: 2. Of those that a mesh axis runs over, the one named last changes fastest.
Arguments:
- left_projection: bfloat16 [128, 512, 32], P('col', 'row'), may hold values from -6 to 6
- right_projection: bfloat16 [128, 512, 32], P('row', 'col'), may hold values from -6 to 6
- output_weight: bfloat16 [1024, 128], replicated, may hold values from -0.1875 to 0.1875
- pair_update_gradient: bfloat16 [512, 512, 128], P('row', 'col'), may hold values from -6 to 6
- alignment_mask: int32 [128, 512], replicated, may hold values from 0 to 1, as said below
Outputs:
- first_factor_derivative: bfloat16 [128, 512, 32], P('col', 'row')
- grad_right: bfloat16 [128, 512, 32], P('row', 'col')
- grad_wout: float32 [1024, 128], replicated
- grad_bias: float32 [128], replicated
Inputs may be any that keep to these rules, and one draw needn't show every extreme that they name: `alignment_mask`: the last residues of the crop, from 1 to 4 of them, are 0 in every 128 row.
All inputs are finite; a program needn't handle non-finite values.
Results may differ from a plain program's by a relative error of at most 0.0058.
Values may be sent and summed in bfloat16 or wider, within the bound.
No kernel may reach another device: no remote copies, remote signals or barrier semaphores. Data moves between devices by JAX's collectives and lax.ppermute only.
A program may use at most 64 MiB of HBM per device.

v0:
```python
import jax
import jax.numpy as jnp
from jax import lax
from jax.sharding import PartitionSpec as P


def per_device(
    left_projection, right_projection, output_weight, pair_update_gradient, alignment_mask
):
    block_row_span, block_column_span, pair_width = pair_update_gradient.shape
    channel_total = left_projection.shape[2]
    alignment_row_total = alignment_mask.shape[0]
    row_start = lax.axis_index("row") * block_row_span
    column_start = lax.axis_index("col") * block_column_span
    mask_row_view = lax.dynamic_slice_in_dim(alignment_mask, row_start, block_row_span, 1).astype(
        jnp.bfloat16
    )
    mask_column_view = lax.dynamic_slice_in_dim(
        alignment_mask, column_start, block_column_span, 1
    ).astype(jnp.bfloat16)
    counts = jnp.dot(mask_row_view.T, mask_column_view, preferred_element_type=jnp.float32)
    scaled_f = pair_update_gradient.astype(jnp.float32) / jnp.maximum(counts, 1.0)[:, :, None]
    bias_sum = jnp.sum(scaled_f, axis=(0, 1))
    scaled = scaled_f.astype(jnp.bfloat16)
    left_full = lax.all_gather(left_projection, "col", axis=0, tiled=True)
    right_full = lax.all_gather(right_projection, "row", axis=0, tiled=True)
    masked_left_rows = left_full * mask_row_view[:, :, None]
    right_masked = right_full * mask_column_view[:, :, None]
    rows_per_block = 8
    number_of_blocks = block_row_span // rows_per_block
    pair_blocks = scaled.reshape(number_of_blocks, rows_per_block * block_column_span, pair_width)
    left_row_blocks = masked_left_rows.reshape(
        alignment_row_total, number_of_blocks, rows_per_block, channel_total
    ).transpose(1, 0, 2, 3)

    def block_step(totals, pieces):
        weight_sum, right_sum = totals
        pair_flat, left_block = pieces
        grad_outer = jnp.einsum(
            "pk,ok->po", pair_flat, output_weight, preferred_element_type=jnp.float32
        ).astype(jnp.bfloat16)
        grad_outer = grad_outer.reshape(
            rows_per_block, block_column_span, channel_total, channel_total
        )
        outer_tile = jnp.einsum(
            "sic,sjd->ijcd", left_block, right_masked, preferred_element_type=jnp.float32
        ).astype(jnp.bfloat16)
        outer_flat = outer_tile.reshape(
            rows_per_block * block_column_span, channel_total * channel_total
        )
        weight_sum = weight_sum + jnp.einsum(
            "po,pk->ok", outer_flat, pair_flat, preferred_element_type=jnp.float32
        )
        left_grad = jnp.einsum(
            "ijcd,sjd->sic", grad_outer, right_masked, preferred_element_type=jnp.float32
        )
        right_sum = right_sum + jnp.einsum(
            "ijcd,sic->sjd", grad_outer, left_block, preferred_element_type=jnp.float32
        )
        return ((weight_sum, right_sum), left_grad)

    starting_carry = (
        jnp.zeros((channel_total * channel_total, pair_width), jnp.float32),
        jnp.zeros((alignment_row_total, block_column_span, channel_total), jnp.float32),
    )
    totals, first_factor_portions = lax.scan(
        block_step, starting_carry, (pair_blocks, left_row_blocks)
    )
    weight_sum, right_sum = totals
    first_factor_summands = first_factor_portions.transpose(1, 0, 2, 3).reshape(
        alignment_row_total, block_row_span, channel_total
    )
    first_factor_reduced = lax.psum_scatter(
        first_factor_summands, "col", scatter_dimension=0, tiled=True
    )
    left_share = first_factor_reduced.shape[0]
    left_mask = lax.dynamic_slice_in_dim(
        mask_row_view, lax.axis_index("col") * left_share, left_share, 0
    )
    first_factor_derivative = (first_factor_reduced * left_mask[:, :, None]).astype(jnp.bfloat16)
    right_summed = lax.psum_scatter(right_sum, "row", scatter_dimension=0, tiled=True)
    right_share = right_summed.shape[0]
    right_mask = lax.dynamic_slice_in_dim(
        mask_column_view, lax.axis_index("row") * right_share, right_share, 0
    )
    grad_right = (right_summed * right_mask[:, :, None]).astype(jnp.bfloat16)
    grad_wout, grad_bias = lax.psum((weight_sum, bias_sum), ("row", "col"))
    return (first_factor_derivative, grad_right, grad_wout, grad_bias)


def solution(mesh):
    return jax.shard_map(
        per_device,
        mesh=mesh,
        in_specs=(P("col", "row", None), P("row", "col", None), P(), P("row", "col", None), P()),
        out_specs=(P("col", "row", None), P("row", "col", None), P(), P()),
        check_vma=False,
    )
```

profile of v0, /device:TPU:1, one launch (start us, length us, event | category | flops | bytes accessed | tf_op | source)
XLA Modules:
  0.0 444.6 jit_solution(8002552018253836575)
XLA Ops:
  8.0 0.0 copy-start
  8.0 0.0 reduce-scatter.3.cloned.1.call-start
  8.1 1.0 dynamic-slice_convert_fusion
  9.0 0.0 copy-start.1
  9.0 0.1 copy.40
  9.1 0.9 constant_dynamic-slice_fusion.1
  10.1 0.1 copy.60
  10.1 0.0 copy-start.2
  10.1 0.1 convolution_maximum_fusion
  10.3 1.6 fusion.11
  11.9 0.0 copy-done.1
  11.9 0.0 copy-done.2
  11.9 0.0 copy-done
  11.9 0.4 convolution_convert_fusion
  12.3 0.5 copy.43
  12.9 1.1 reshape.28
  14.0 98.9 %all_gather.6 = bf16[128,64,32]{1,2,0:T(8,128)(2,1)} all-gather(bf16[2,64,32]{1,2,0:T(8,128)(2,1)} %param.6), channel_id=1, replica_groups=mesh['row'=64,'col'=8] {'row'}, dimensions={0}, use_global_device_ids=true | all-gather | bytes 532480 | tf_op jit(solution)/shard_map/all_gather | solution.py:26
  112.8 2.8 copy.41
  115.7 4.8 %copy.52 = bf16[8,64,32,32]{2,3,1,0:T(8,128)(2,1)} copy(bf16[8,64,32,32]{1,0,3,2:T(8,128)(2,1)S(1)} %reshape.28) | data formatting | bytes 2097152 | tf_op jit(solution)/shard_map/while/body/eval_jaxpr/reshape | solution.py:42
  120.5 3.7 convolution_bitcast_fusion
  124.2 0.0 reduce-scatter.3.cloned.1.call-update
  124.2 0.0 reduce-scatter.5.cloned.1.call-start
  124.3 0.0 copy-done.5
  124.3 23.7 %all_gather.7 = bf16[128,8,32]{2,1,0:T(8,128)(2,1)S(1)} all-gather(bf16[16,8,32]{2,1,0:T(8,128)(2,1)S(1)} %copy-done.5), channel_id=1, replica_groups=mesh['row'=64,'col'=8] {'col'}, dimensions={0}, use_global_device_ids=true | all-gather | bytes 73728 | tf_op jit(solution)/shard_map/all_gather | solution.py:25
  148.0 0.2 copy.46
  148.2 0.0 copy-done.3
  148.2 2.4 fusion.2
  150.6 4.0 copy.48
  154.7 0.0 reduce-scatter.5.cloned.1.call-update
  154.7 0.2 all-reduce.2.cloned.1.call-start
  154.9 3.2 convert_bitcast_fusion
  158.1 7.8 %copy.49 = bf16[8,64,32,32]{1,0,3,2:T(8,128)(2,1)S(1)} copy(bf16[8,64,32,32]{2,3,0,1:T(8,128)(2,1)} %convert_bitcast_fusion) | data formatting | bytes 2097152 | tf_op jit(solution)/shard_map/while/body/eval_jaxpr/convert_element_type | solution.py:47
  165.9 0.0 copy-start.4
  165.9 0.0 copy-start.6
  166.0 1.3 reshape.29
  167.2 1.2 fusion.20
  168.5 0.0 all-reduce.2.cloned.1.call-update
  168.5 0.7 fusion.19
  169.2 0.0 copy-done.4
  169.2 0.1 dynamic-slice_convert_fusion.1
  169.3 0.0 copy-done.6
  169.3 100.3 %psum.15 = f32[128]{0:T(128)} all-reduce(f32[128]{0:T(128)S(1)} %copy-done.6), channel_id=1, replica_groups=mesh['row'=64,'col'=8] {'row','col'}, use_global_device_ids=true, to_apply=%region_4.5 | all-reduce | flops 128 | bytes 1024 | tf_op jit(solution)/shard_map/psum | solution.py:87
  269.5 0.9 multiply_convert_fusion
  270.5 0.6 copy.50
  271.1 37.8 %reduce-scatter.5.cloned.1.call-done = f32[2,64,32]{1,2,0:T(8,128)} async-done(((f32[128,64,32]{1,2,0:T(8,128)}), f32[2,64,32]{1,2,0:T(8,128)}) %reduce-scatter.5.cloned.1.call-update) | async-done | bytes 16400 | tf_op jit(solution)/shard_map/reduce_scatter | solution.py:81
  308.9 1.4 multiply_convert_fusion.1
  310.3 125.0 %all-reduce.2.cloned.1.call-done = f32[1024,128]{1,0:T(8,128)} async-done(((f32[1024,128]{1,0:T(8,128)}), f32[1024,128]{1,0:T(8,128)}) %all-reduce.2.cloned.1.call-update) | async-done | bytes 524304 | tf_op jit(solution)/shard_map/psum | solution.py:87
  435.2 1.9 copy.66
  (4 shorter events, 0.0 us)
Async XLA Ops:
  8.0 3.9 copy-start
  8.0 261.5 %reduce-scatter.3.cloned.1.call-start = ((), (), s32[]{:S(2)}) async-start(), calls=%async_computation.2 | async-start | bytes 589824 | tf_op jit(solution)/shard_map/reduce_scatter | solution.py:73
  9.0 2.8 copy-start.1
  10.1 1.7 copy-start.2
  120.5 3.8 copy-start.5
  120.5 27.8 %copy-start.3 = (bf16[128,8]{0,1:T(8,128)(2,1)S(1)}, bf16[128,8]{0,1:T(8,128)(2,1)}, u32[]{:S(2)}) copy-start(bf16[128,8]{0,1:T(8,128)(2,1)} %copy-done.2) | copy-start | bytes 6148
  124.2 184.7 %reduce-scatter.5.cloned.1.call-start = ((), (), s32[]{:S(2)}) async-start(), calls=%async_computation.3 | async-start | bytes 2129920 | tf_op jit(solution)/shard_map/reduce_scatter | solution.py:81
  154.7 280.6 %all-reduce.2.cloned.1.call-start = ((), (), s32[]{:S(2)}) async-start(), calls=%async_computation.4 | async-start | bytes 1048576 | tf_op jit(solution)/shard_map/psum | solution.py:87
  165.9 3.2 copy-start.4
  165.9 3.3 copy-start.6
Sparse Core Ops, SparseCore 0:
  124.3 28.9 reduce-scatter.2
  158.7 150.1 reduce-scatter.4
Sparse Core Ops, SparseCore 1:
  168.6 266.6 all-reduce.1
where the time goes:
time: 445 us
  blocking collectives  223 us (50%)
  waiting for transfers between devices  163 us (37%)
  local copies, waits for them, and re-layouts  26.1 us (6%)
  between operations  15.6 us (4%)
  matrix products  11.2 us (3%)
  other arithmetic  5.59 us (1%)
    psum x1, waiting for transfers between devices, per_device(): grad_wout, grad_bias = lax.psum((weight_sum, bias_sum), ('row', 'col'))  125 us
    psum x1, blocking collectives, per_device(): grad_wout, grad_bias = lax.psum((weight_sum, bias_sum), ('row', 'col'))  100 us
    all_gather x1, blocking collectives, per_device(): right_full = lax.all_gather(right_projection, 'row', axis=0, tiled=True)  98.9 us
    reduce_scatter x1, waiting for transfers between devices, per_device(): lax.psum_scatter(right_sum, 'row', scatter_dimension=0, tiled=True)  37.8 us
    all_gather x1, blocking collectives, per_device(): left_full = lax.all_gather(left_projection, 'col', axis=0, tiled=True)  23.7 us
  transfers between devices with their start and end apart: 3, of which 2 were waited for; matrix products, arithmetic and copies ran while one was open for 5% of the time, Pallas kernels for 0%

commit v1 on v0

--- a/solution.py
+++ b/solution.py
@@ -22,7 +22,8 @@
     scaled_f = pair_update_gradient.astype(jnp.float32) / jnp.maximum(counts, 1.0)[:, :, None]
     bias_sum = jnp.sum(scaled_f, axis=(0, 1))
     scaled = scaled_f.astype(jnp.bfloat16)
-    left_full = lax.all_gather(left_projection, "col", axis=0, tiled=True)
+    outgoing = jnp.stack([left_projection] * lax.axis_size("col"))
+    left_full = jnp.concatenate(lax.all_to_all(outgoing, "col", 0, 0), axis=0)
     right_full = lax.all_gather(right_projection, "row", axis=0, tiled=True)
     masked_left_rows = left_full * mask_row_view[:, :, None]
     right_masked = right_full * mask_column_view[:, :, None]

time: 445 us -> 527 us (1.18)
  waiting for transfers between devices: 163 us -> 260 us
  blocking collectives: 223 us -> 194 us
  starting transfers between devices: 0.3 us -> 5.98 us
    psum x1, waiting for transfers between devices: 125 us -> 197 us  [per_device(): grad_wout, grad_bias = lax.psum((weight_sum, bias_sum), ('row', 'col'))]
    reduce_scatter x1, waiting for transfers between devices: 37.8 us -> 63.6 us  [per_device(): lax.psum_scatter(right_sum, 'row', scatter_dimension=0, tiled=True)]
    all_gather x1 -> x0, blocking collectives: 23.7 us -> none  [per_device(): left_full = lax.all_gather(left_projection, 'col', axis=0, tiled=True)]
    all_to_all x0 -> x1, starting transfers between devices: none -> 5.86 us  [per_device(): left_full = jnp.concatenate(lax.all_to_all(outgoing, 'col', 0, 0), axis=0)]
  transfers between devices with their start and end apart: 3 -> 4, of which waited for: 2 -> 2; matrix products, arithmetic and copies ran while one was open for 5% -> 9% of each run, Pallas kernels for 0% -> 0%
where the time goes in v1:
time: 527 us; the launch traced here: 526 us
  waiting for transfers between devices  260 us (49%)
  blocking collectives  194 us (37%)
  local copies, waits for them, and re-layouts  31.3 us (6%)
  between operations  15.7 us (3%)
  matrix products  11.1 us (2%)
  other arithmetic  7.7 us (1%)
  starting transfers between devices  5.98 us (1%)
    psum x1, waiting for transfers between devices, per_device(): grad_wout, grad_bias = lax.psum((weight_sum, bias_sum), ('row', 'col'))  197 us
    psum x1, blocking collectives, per_device(): grad_wout, grad_bias = lax.psum((weight_sum, bias_sum), ('row', 'col'))  96.9 us
    all_gather x1, blocking collectives, per_device(): right_full = lax.all_gather(right_projection, 'row', axis=0, tiled=True)  96.9 us
    reduce_scatter x1, waiting for transfers between devices, per_device(): lax.psum_scatter(right_sum, 'row', scatter_dimension=0, tiled=True)  63.6 us
  transfers between devices with their start and end apart: 4, of which 2 were waited for; matrix products, arithmetic and copies ran while one was open for 9% of the time, Pallas kernels for 0%

profile of v1, /device:TPU:1, one launch (start us, length us, event | category | flops | bytes accessed | tf_op | source)
XLA Modules:
  0.0 526.0 jit_solution(12431251294752907039)
XLA Ops:
  8.0 0.0 copy-start
  8.0 0.8 stack.2
  8.8 0.9 reshape.42
  9.7 5.9 %all-to-all-start = ((bf16[8,2,2048]{2,1,0:T(2,128)(2,1)}), bf16[8,2,2048]{2,1,0:T(2,128)(2,1)S(1)}, u32[]{:S(2)}, u32[]{:S(2)}) async-start(bf16[8,2,2048]{2,1,0:T(2,128)(2,1)} %reshape.42), calls=%async_computation.1 | async-start | bytes 131072 | tf_op jit(solution)/shard_map/all_to_all | solution.py:26
  15.6 0.0 reduce-scatter.3.cloned.1.call-start
  15.7 0.9 dynamic-slice_convert_fusion
  16.6 0.0 copy-start.1
  16.6 0.1 copy.40
  16.7 0.9 constant_dynamic-slice_fusion.1
  17.6 0.1 copy.62
  17.7 0.1 convolution_maximum_fusion
  17.8 1.6 fusion.11
  19.4 0.0 copy-done.1
  19.4 0.0 copy-done
  19.4 0.4 convolution_convert_fusion
  19.9 1.3 copy.43
  21.2 2.8 reshape.33
  24.0 96.9 %all_gather.3 = bf16[128,64,32]{1,2,0:T(8,128)(2,1)} all-gather(bf16[2,64,32]{1,2,0:T(8,128)(2,1)S(1)} %copy-done.4), channel_id=1, replica_groups=mesh['row'=64,'col'=8] {'row'}, dimensions={0}, use_global_device_ids=true | all-gather | bytes 532480 | tf_op jit(solution)/shard_map/all_gather | solution.py:27
  120.9 2.8 copy.41
  123.7 4.8 copy.54
  128.5 3.7 convolution_bitcast_fusion
  132.2 0.0 reduce-scatter.3.cloned.1.call-update
  132.3 0.0 reduce-scatter.5.cloned.1.call-start
  132.3 0.7 copy.46
  133.1 0.0 all-to-all-done
  133.1 0.2 reshape.43
  133.2 1.0 bitcast_multiply_fusion
  134.2 0.2 copy.47
  134.4 2.4 fusion.2
  136.8 4.1 copy.49
  140.9 0.0 reduce-scatter.5.cloned.1.call-update
  140.9 0.0 all-reduce.2.cloned.1.call-start
  141.0 96.9 %psum.15 = f32[128]{0:T(128)} all-reduce(f32[128]{0:T(128)S(1)} %copy-done.7), channel_id=1, replica_groups=mesh['row'=64,'col'=8] {'row','col'}, use_global_device_ids=true, to_apply=%region_4.5 | all-reduce | flops 128 | bytes 1024 | tf_op jit(solution)/shard_map/psum | solution.py:88
  237.9 1.3 fusion.15
  239.1 0.7 dynamic-slice_convert_fusion.1
  239.8 3.2 convert_bitcast_fusion
  243.0 7.8 %copy.51 = bf16[8,64,32,32]{1,0,3,2:T(8,128)(2,1)S(1)} copy(bf16[8,64,32,32]{2,3,0,1:T(8,128)(2,1)} %convert_bitcast_fusion) | data formatting | bytes 2097152 | tf_op jit(solution)/shard_map/while/body/eval_jaxpr/convert_element_type | solution.py:48
  250.8 0.0 copy-start.5
  250.8 1.3 reshape.35
  252.1 1.2 fusion.16
  253.3 0.0 all-reduce.2.cloned.1.call-update
  253.3 0.0 reduce-scatter.3.cloned.1.call-done
  253.4 0.9 multiply_convert_fusion
  254.3 0.6 copy.52
  254.9 63.6 %reduce-scatter.5.cloned.1.call-done = f32[2,64,32]{1,2,0:T(8,128)} async-done(((f32[128,64,32]{1,2,0:T(8,128)}), f32[2,64,32]{1,2,0:T(8,128)}) %reduce-scatter.5.cloned.1.call-update) | async-done | bytes 16400 | tf_op jit(solution)/shard_map/reduce_scatter | solution.py:82
  318.5 1.4 multiply_convert_fusion.1
  319.9 196.8 %all-reduce.2.cloned.1.call-done = f32[1024,128]{1,0:T(8,128)} async-done(((f32[1024,128]{1,0:T(8,128)}), f32[1024,128]{1,0:T(8,128)}) %all-reduce.2.cloned.1.call-update) | async-done | bytes 524304 | tf_op jit(solution)/shard_map/psum | solution.py:88
  516.7 1.9 copy.68
  (12 shorter events, 0.0 us)
Async XLA Ops:
  8.0 11.4 %copy-start = (bf16[1024,128]{1,0:T(8,128)(2,1)S(1)}, bf16[1024,128]{1,0:T(8,128)(2,1)}, u32[]{:S(2)}) copy-start(bf16[1024,128]{1,0:T(8,128)(2,1)} %param.7) | copy-start | bytes 786436
  9.7 123.3 %all-to-all-start = ((bf16[8,2,2048]{2,1,0:T(2,128)(2,1)}), bf16[8,2,2048]{2,1,0:T(2,128)(2,1)S(1)}, u32[]{:S(2)}, u32[]{:S(2)}) async-start(bf16[8,2,2048]{2,1,0:T(2,128)(2,1)} %reshape.42), calls=%async_computation.1 | async-start | bytes 131072 | tf_op jit(solution)/shard_map/all_to_all | solution.py:26
  15.6 237.8 %reduce-scatter.3.cloned.1.call-start = ((), (), s32[]{:S(2)}) async-start(), calls=%async_computation.3 | async-start | bytes 589824 | tf_op jit(solution)/shard_map/reduce_scatter | solution.py:74
  16.6 2.8 copy-start.1
  17.7 114.6 %copy-start.2 = (bf16[128,8]{0,1:T(8,128)(2,1)}, bf16[128,8]{0,1:T(8,128)(2,1)S(1)}, u32[]{:S(2)}) copy-start(bf16[128,8]{0,1:T(8,128)(2,1)S(1)} %convert_element_type.39) | copy-start | bytes 6148
  21.2 2.8 copy-start.4
  132.3 186.2 %reduce-scatter.5.cloned.1.call-start = ((), (), s32[]{:S(2)}) async-start(), calls=%async_computation.4 | async-start | bytes 2129920 | tf_op jit(solution)/shard_map/reduce_scatter | solution.py:82
  136.8 4.1 copy-start.7
  136.8 102.3 %copy-start.3 = (bf16[128,8]{0,1:T(8,128)(2,1)S(1)}, bf16[128,8]{0,1:T(8,128)(2,1)}, u32[]{:S(2)}) copy-start(bf16[128,8]{0,1:T(8,128)(2,1)} %copy-done.2) | copy-start | bytes 6148
  140.9 375.8 %all-reduce.2.cloned.1.call-start = ((), (), s32[]{:S(2)}) async-start(), calls=%async_computation.5 | async-start | bytes 1048576 | tf_op jit(solution)/shard_map/psum | solution.py:88
  250.8 2.6 copy-start.5
  250.8 67.7 %copy-start.6 = (f32[2,64]{1,0:T(2,128)S(1)}, f32[2,64]{1,0:T(2,128)}, u32[]{:S(2)}) copy-start(f32[2,64]{1,0:T(2,128)} %fusion.15) | copy-start | bytes 1540
Sparse Core Ops, SparseCore 0:
  132.4 30.2 reduce-scatter.2
  168.0 150.4 reduce-scatter.4
Sparse Core Ops, SparseCore 1:
  253.4 263.2 all-reduce.1

commit v2 on v0

--- a/solution.py
+++ b/solution.py
@@ -1,7 +1,17 @@
+import functools
 import jax
 import jax.numpy as jnp
 from jax import lax
 from jax.sharding import PartitionSpec as P
+
+
+def link_ranges(base_x, net_axis, axis_tag):
+    for ix in (axis_tag, net_axis):
+        base_x = lax.psum(base_x, ix)
+    return base_x
+
+
+start_edges = functools.partial(link_ranges, net_axis="col", axis_tag="row")
 
 
 def per_device(
@@ -84,7 +94,7 @@
         mask_column_view, lax.axis_index("row") * right_share, right_share, 0
     )
     grad_right = (right_summed * right_mask[:, :, None]).astype(jnp.bfloat16)
-    grad_wout, grad_bias = lax.psum((weight_sum, bias_sum), ("row", "col"))
+    grad_wout, grad_bias = start_edges((weight_sum, bias_sum))
     return (first_factor_derivative, grad_right, grad_wout, grad_bias)
 
 

time: 445 us -> 785 us (1.76)
  waiting for transfers between devices: 163 us -> 444 us
  blocking collectives: 223 us -> 277 us
    psum x1 -> x2, waiting for transfers between devices: 125 us -> 444 us  [link_ranges(): base_x = lax.psum(base_x, ix)]
    psum x1 -> x2, blocking collectives: 100 us -> 155 us  [link_ranges(): base_x = lax.psum(base_x, ix)]
    reduce_scatter x1, waiting for transfers between devices: 37.8 us -> 0.01 us  [per_device(): lax.psum_scatter(right_sum, 'row', scatter_dimension=0, tiled=True)]
  transfers between devices with their start and end apart: 3 -> 4, of which waited for: 2 -> 2; matrix products, arithmetic and copies ran while one was open for 5% -> 3% of each run, Pallas kernels for 0% -> 0%
where the time goes in v2:
time: 785 us; the launch traced here: 781 us
  waiting for transfers between devices  444 us (57%)
  blocking collectives  277 us (35%)
  local copies, waits for them, and re-layouts  28.2 us (4%)
  between operations  15.8 us (2%)
  matrix products  12.4 us (2%)
    psum x2, waiting for transfers between devices, link_ranges(): base_x = lax.psum(base_x, ix)  444 us
    psum x2, blocking collectives, link_ranges(): base_x = lax.psum(base_x, ix)  155 us
    all_gather x1, blocking collectives, per_device(): right_full = lax.all_gather(right_projection, 'row', axis=0, tiled=True)  98.5 us
    all_gather x1, blocking collectives, per_device(): left_full = lax.all_gather(left_projection, 'col', axis=0, tiled=True)  23.5 us
  transfers between devices with their start and end apart: 4, of which 2 were waited for; matrix products, arithmetic and copies ran while one was open for 3% of the time, Pallas kernels for 0%

profile of v2, /device:TPU:1, one launch (start us, length us, event | category | flops | bytes accessed | tf_op | source)
XLA Modules:
  0.0 780.6 jit_solution(8008193621182842589)
XLA Ops:
  8.0 0.0 copy-start
  8.0 0.0 all-reduce.3.cloned.1.call-start
  8.1 1.0 dynamic-slice_convert_fusion
  9.0 0.1 copy.40
  9.1 0.9 constant_dynamic-slice_fusion.1
  10.1 0.1 copy.60
  10.1 0.1 convolution_maximum_fusion
  10.3 23.5 %all_gather.7 = bf16[128,8,32]{2,1,0:T(8,128)(2,1)S(1)} all-gather(bf16[16,8,32]{2,1,0:T(8,128)(2,1)} %param.5), channel_id=1, replica_groups=mesh['row'=64,'col'=8] {'col'}, dimensions={0}, use_global_device_ids=true | all-gather | bytes 73728 | tf_op jit(solution)/shard_map/all_gather | solution.py:35
  33.8 0.2 copy.46
  34.0 98.5 %all_gather.6 = bf16[128,64,32]{1,2,0:T(8,128)(2,1)S(1)} all-gather(bf16[2,64,32]{1,2,0:T(8,128)(2,1)} %param.6), channel_id=1, replica_groups=mesh['row'=64,'col'=8] {'row'}, dimensions={0}, use_global_device_ids=true | all-gather | bytes 532480 | tf_op jit(solution)/shard_map/all_gather | solution.py:36
  132.4 1.5 copy.41
  134.0 3.2 convert_bitcast_fusion
  137.2 7.8 copy.49
  145.0 0.0 copy-start.1
  145.0 2.1 reshape.29
  147.1 0.0 copy-done.1
  147.1 0.2 fusion.11
  147.2 2.5 fusion.20
  149.7 0.0 all-reduce.3.cloned.1.call-update
  149.8 0.0 reduce-scatter.3.cloned.1.call-start
  149.8 0.0 copy-done
  149.8 0.4 convolution_convert_fusion
  150.3 1.3 copy.43
  151.6 2.8 reshape.28
  154.4 4.8 copy.52
  159.2 3.7 convolution_bitcast_fusion
  162.9 0.0 reduce-scatter.3.cloned.1.call-update
  162.9 0.2 reduce-scatter.5.cloned.1.call-start
  163.2 2.4 fusion.2
  165.6 4.1 copy.48
  169.7 0.0 reduce-scatter.5.cloned.1.call-update
  169.7 0.0 all-reduce.5.cloned.1.call-start
  169.7 138.5 %psum.30 = f32[128]{0:T(128)S(1)} all-reduce(f32[128]{0:T(128)S(1)} %get-tuple-element.44), channel_id=1, replica_groups=mesh['row'=64,'col'=8] {'row'}, use_global_device_ids=true, to_apply=%region_5.6 | all-reduce | flops 128 | bytes 1024 | tf_op jit(solution)/shard_map/psum | solution.py:10
  308.2 16.2 %psum.31 = f32[128]{0:T(128)} all-reduce(f32[128]{0:T(128)S(1)} %psum.30), channel_id=1, replica_groups=mesh['row'=64,'col'=8] {'col'}, use_global_device_ids=true, to_apply=%region_6.7 | all-reduce | flops 128 | bytes 1024 | tf_op jit(solution)/shard_map/psum | solution.py:10
  324.4 0.1 dynamic-slice_convert_fusion.1
  324.5 369.7 %all-reduce.3.cloned.1.call-done = f32[1024,128]{1,0:T(8,128)} async-done(((f32[1024,128]{1,0:T(8,128)}), f32[1024,128]{1,0:T(8,128)}) %all-reduce.3.cloned.1.call-update) | async-done | bytes 524304 | tf_op jit(solution)/shard_map/psum | solution.py:10
  694.3 0.0 all-reduce.5.cloned.1.call-update
  694.3 0.0 reduce-scatter.3.cloned.1.call-done
  694.3 0.9 multiply_convert_fusion
  695.3 0.6 copy.50
  695.9 0.0 reduce-scatter.5.cloned.1.call-done
  695.9 1.4 multiply_convert_fusion.1
  697.3 73.9 %all-reduce.5.cloned.1.call-done = f32[1024,128]{1,0:T(8,128)} async-done(((f32[1024,128]{1,0:T(8,128)}), f32[1024,128]{1,0:T(8,128)}) %all-reduce.5.cloned.1.call-update) | async-done | bytes 524304 | tf_op jit(solution)/shard_map/psum | solution.py:10
  771.1 1.9 copy.67
  (2 shorter events, 0.0 us)
Async XLA Ops:
  8.0 141.8 %copy-start = (bf16[1024,128]{1,0:T(8,128)(2,1)S(1)}, bf16[1024,128]{1,0:T(8,128)(2,1)}, u32[]{:S(2)}) copy-start(bf16[1024,128]{1,0:T(8,128)(2,1)} %param.7) | copy-start | bytes 786436
  8.0 686.2 %all-reduce.3.cloned.1.call-start = ((), (), s32[]{:S(2)}) async-start(), calls=%async_computation.4 | async-start | bytes 1048576 | tf_op jit(solution)/shard_map/psum | solution.py:10
  145.0 2.1 copy-start.1
  149.8 544.6 %reduce-scatter.3.cloned.1.call-start = ((), (), s32[]{:S(2)}) async-start(), calls=%async_computation.2 | async-start | bytes 589824 | tf_op jit(solution)/shard_map/reduce_scatter | solution.py:83
  162.9 533.0 %reduce-scatter.5.cloned.1.call-start = ((), (), s32[]{:S(2)}) async-start(), calls=%async_computation.3 | async-start | bytes 2129920 | tf_op jit(solution)/shard_map/reduce_scatter | solution.py:91
  169.7 601.4 %all-reduce.5.cloned.1.call-start = ((), (), s32[]{:S(2)}) async-start(), calls=%async_computation.5 | async-start | bytes 1048576 | tf_op jit(solution)/shard_map/psum | solution.py:10
Sparse Core Ops, SparseCore 0:
  149.9 544.3 all-reduce.2
Sparse Core Ops, SparseCore 1:
  163.0 29.0 reduce-scatter.2
  197.2 150.5 reduce-scatter.4
  694.4 76.7 all-reduce.4
